TPU v7x, 32 devices: a whole 2x2x4 slice. The times are simulated.
32 devices in a mesh: band: 8 (over z, y), lev: 4 (over x, core).
Axes of the slice: x: 2, y: 2, z: 4, core: 2. Of those that a mesh axis runs over, the one named last changes fastest.
Arguments:
- spectral: float32 [672, 16, 128], P('band', 'lev'), may hold values from -6 to 6
- legendre: bfloat16 [672, 64, 128], P('band'), may hold values from -0.15625 to 0.15625
- wave_ids: int32 [64], P('band'), may hold values from 0 to 1279, as said below
- block_slot: int32 [672], P('band'), may hold values from 0 to 7, as said below
- block_start: int32 [672], P('band'), may hold values from 0 to 1216, as said below
- lat_weights: float32 [128], replicated, may hold values from 0.5 to 2
- drag: float32 [16, 2, 128], P('lev'), may hold values from 0.1 to 1
- mode_inverse: float32 [16, 16], replicated, may hold values from -1.5 to 1.5
- level_modes: float32 [16, 16], replicated, may hold values from -1.5 to 1.5
- depths: float32 [16], replicated, may hold values from 0.1 to 3
Outputs:
- spectral_next: float32 [672, 16, 128], P('band', 'lev')
Inputs may be any that keep to these rules, and one draw needn't show every extreme that they name: `wave_ids`: distinct wavenumbers. The slots of index b of band, entries b * 8 to (b + 1) * 8 - 1, hold 4 pairs m and 1279 - m in some order; the pair 0 and 1279 is always present. `block_slot`: blocks b * 84 to (b + 1) * 84 - 1 belong to index b of band. For each slot of index b with wavenumber m there is exactly one block with each start 0, 64, 128, ... below 1280 - m, and no other block; the blocks stand in no particular order. `block_start`: A multiple of 64; see block_slot.
All inputs are finite; a program needn't handle non-finite values.
Results may differ from a plain program's by a relative error of at most 0.009.
Values may be sent and summed in bfloat16 or wider, within the bound.
A program may use at most 128 MiB of HBM per device.

v0:
```python
import math

import jax
import jax.numpy as jnp
from jax import lax
from jax.sharding import PartitionSpec as P

NTRUNC = 1280
NLON = 4096
LAT_DEV = 16


def row_offsets(row_count):
    half_rows = row_count // 2
    positions = jnp.arange(row_count, dtype=jnp.int32)
    return jnp.where(positions < half_rows, 2 * positions, 2 * (positions - half_rows) + 1)


def block_degrees(wave_ids, block_slot, block_start, row_count):
    slot_ids = jnp.arange(wave_ids.shape[0], dtype=jnp.int32)
    matches = block_slot[:, None] == slot_ids[None, :]
    wave_of_block = jnp.sum(jnp.where(matches, wave_ids[None, :], 0), axis=1)
    degree = wave_of_block[:, None] + block_start[:, None] + row_offsets(row_count)[None, :]
    return (matches, degree)


def drag_columns(incoming, all_waves):
    wave_count = all_waves.shape[0]
    spectra = incoming.reshape(wave_count, 2, -1)
    stacked = jnp.concatenate([spectra[:, 0, :], spectra[:, 1, :]], axis=0)
    block_width = min(NLON, 512)
    block_turns = NLON // block_width
    contract = (((0,), (0,)), ((), ()))

    def one_block(block_index, running):
        first = block_index * block_width
        points = first + jnp.arange(block_width, dtype=jnp.int32)
        phases = points[:, None] * all_waves[None, :] % NLON
        angles = phases.astype(jnp.float32) * (2.0 * math.pi / NLON)
        twiddle = jnp.concatenate([jnp.cos(angles), -jnp.sin(angles)], axis=1)
        high_rows = twiddle.astype(jnp.bfloat16)
        low_rows = (twiddle - high_rows.astype(jnp.float32)).astype(jnp.bfloat16)
        grid_values = jnp.dot(high_rows, stacked, preferred_element_type=jnp.float32) + jnp.dot(
            low_rows, stacked, preferred_element_type=jnp.float32
        )
        grid_values = grid_values / math.sqrt(wave_count)
        drag_force = grid_values * jnp.abs(grid_values)
        force_high = drag_force.astype(jnp.bfloat16)
        force_low = (drag_force - force_high.astype(jnp.float32)).astype(jnp.bfloat16)
        summed = lax.dot_general(
            high_rows, force_high, contract, preferred_element_type=jnp.float32
        )
        summed = summed + lax.dot_general(
            high_rows, force_low, contract, preferred_element_type=jnp.float32
        )
        summed = summed + lax.dot_general(
            low_rows, force_high, contract, preferred_element_type=jnp.float32
        )
        return running + summed

    summed = lax.fori_loop(
        0, block_turns, one_block, jnp.zeros((2 * wave_count, stacked.shape[1]), jnp.float32)
    )
    summed = summed / math.sqrt(NLON)
    result = jnp.stack([summed[:wave_count], summed[wave_count:]], axis=1)
    return result.astype(jnp.bfloat16).reshape(incoming.shape)


def on_device(
    spectral,
    legendre,
    wave_ids,
    block_slot,
    block_start,
    lat_weights,
    drag,
    mode_inverse,
    level_modes,
    depths,
):
    block_count, level_count, columns = spectral.shape
    row_count = legendre.shape[1]
    half_rows = row_count // 2
    lat_pairs = legendre.shape[2]
    groups = lat_pairs // LAT_DEV
    slot_count = wave_ids.shape[0]
    all_levels = mode_inverse.shape[0]
    all_waves = lax.all_gather(wave_ids, "band", axis=0, tiled=True)
    matches, degree = block_degrees(wave_ids, block_slot, block_start, row_count)
    live_rows = (degree < NTRUNC).astype(jnp.float32)
    live_cols = jnp.concatenate([live_rows, live_rows], axis=1)
    masked = spectral * live_cols[:, None, :]
    split_coeff = masked.astype(jnp.bfloat16).reshape(block_count, level_count, 2, 2, half_rows)
    slot_coeff = jnp.where(
        matches[:, :, None, None, None, None], split_coeff[:, None], jnp.zeros((), jnp.bfloat16)
    )
    even_part = jnp.einsum(
        "kslcr,kri->slci",
        slot_coeff[:, :, :, :, 0, :],
        legendre[:, :half_rows, :],
        preferred_element_type=jnp.float32,
    )
    odd_part = jnp.einsum(
        "kslcr,kri->slci",
        slot_coeff[:, :, :, :, 1, :],
        legendre[:, half_rows:, :],
        preferred_element_type=jnp.float32,
    )
    hemispheres = jnp.stack([even_part + odd_part, even_part - odd_part], axis=3)
    hemispheres = hemispheres.reshape(slot_count, level_count, 2, 2, groups, LAT_DEV)
    outgoing = jnp.transpose(hemispheres, (4, 0, 2, 1, 3, 5))
    outgoing = outgoing.reshape(groups, slot_count, 2, level_count * 2 * LAT_DEV).astype(
        jnp.bfloat16
    )
    incoming = lax.all_to_all(outgoing, "band", split_axis=0, concat_axis=1, tiled=True)
    returned = lax.all_to_all(
        drag_columns(incoming, all_waves), "band", split_axis=1, concat_axis=0, tiled=True
    )
    arrived = returned.reshape(groups, slot_count, 2, level_count, 2, LAT_DEV).astype(jnp.float32)
    northern = arrived[:, :, :, :, 0, :]
    southern = arrived[:, :, :, :, 1, :]
    drag_grid = drag.reshape(level_count, 2, groups, LAT_DEV)
    drag_north = jnp.transpose(drag_grid[:, 0], (1, 0, 2))[:, None, None, :, :]
    drag_south = jnp.transpose(drag_grid[:, 1], (1, 0, 2))[:, None, None, :, :]
    weights_grid = lat_weights.reshape(groups, 1, 1, 1, LAT_DEV)
    symmetric = (-weights_grid * (drag_north * northern + drag_south * southern)).astype(
        jnp.bfloat16
    )
    antisymmetric = (-weights_grid * (drag_north * northern - drag_south * southern)).astype(
        jnp.bfloat16
    )
    sym_blocks = jnp.take(symmetric, block_slot, axis=1)
    anti_blocks = jnp.take(antisymmetric, block_slot, axis=1)
    legendre_grid = legendre.reshape(block_count, row_count, groups, LAT_DEV)
    even_tend = jnp.einsum(
        "gkclt,krgt->klcr",
        sym_blocks,
        legendre_grid[:, :half_rows],
        preferred_element_type=jnp.float32,
    )
    odd_tend = jnp.einsum(
        "gkclt,krgt->klcr",
        anti_blocks,
        legendre_grid[:, half_rows:],
        preferred_element_type=jnp.float32,
    )
    tendency = (
        jnp.stack([even_tend, odd_tend], axis=3).reshape(block_count, level_count, columns)
        * live_cols[:, None, :]
    )
    combined = masked + tendency
    degree_f = degree.astype(jnp.float32)
    growth = degree_f * (degree_f + 1.0) / (NTRUNC * NTRUNC)
    growth = jnp.concatenate([growth, growth], axis=1)
    modal_part = jnp.zeros((block_count, all_levels, columns), jnp.float32) + jnp.einsum(
        "al,klx->kax",
        mode_inverse,
        lax.all_gather(combined.astype(jnp.bfloat16), "lev", axis=1, tiled=True).astype(
            jnp.float32
        ),
        precision=lax.Precision.HIGHEST,
    )
    implicit_gain = 1.0 / (1.0 + depths[None, :, None] * growth[:, None, :])
    own_rows = lax.dynamic_slice_in_dim(
        level_modes, lax.axis_index("lev") * level_count, level_count, 0
    )
    result = jnp.einsum(
        "la,kax->klx", own_rows, modal_part * implicit_gain, precision=lax.Precision.HIGHEST
    )
    return result


def solution(mesh):
    placed = (
        P("band", "lev", None),
        P("band", None, None),
        P("band"),
        P("band"),
        P("band"),
        P(),
        P("lev", None, None),
        P(),
        P(),
        P(),
    )
    return jax.shard_map(
        on_device, mesh=mesh, in_specs=placed, out_specs=P("band", "lev", None), check_vma=False
    )
```

profile of v0, /device:TPU:0, one launch (start us, length us, event | category | flops | bytes accessed | tf_op | source)
XLA Modules:
  0.0 85.1 jit_solution(1211475557090044259)
XLA Ops:
  0.0 0.7 iota_compare_fusion
  0.7 0.8 select_reduce_fusion
  1.4 0.7 add.151
  2.4 1.1 %copy.100 = f32[84,4,128]{0,2,1:T(8,128)S(1)} copy(f32[84,4,128]{2,1,0:T(4,128)} %param.14) | data formatting | bytes 344064 | tf_op args[0]
  3.4 1.6 %fusion.35 = (bf16[84,32,128]{2,1,0:T(8,128)(2,1)S(1)}, bf16[84,32,128]{2,1,0:T(8,128)(2,1)S(1)}) fusion(bf16[84,64,128]{2,1,0:T(8,128)(2,1)} %param.15), kind=kLoop, calls=%fused_computation.93 | loop fusion | bytes 2752512 | tf_op jit(solution)/shard_map/slice | solution.py:106
  7.2 0.7 maximum_bitcast_fusion
  7.9 0.8 convert_element_type.110
  8.7 7.3 %all-to-all-start = ((bf16[8,8,2,128]{3,1,2,0:T(8,128)(2,1)}), bf16[8,8,2,128]{3,1,2,0:T(8,128)(2,1)S(1)}, u32[]{:S(2)}, u32[]{:S(2)}) async-start(bf16[8,8,2,128]{3,1,2,0:T(8,128)(2,1)} %convert_element_type.110), calls=%async_computation | async-start | bytes 65536 | tf_op jit(solution)/shard_map/all_to_all | solution.py:115
  16.0 2.6 %copy.113 = bf16[84,64,128]{1,2,0:T(8,128)(2,1)} copy(bf16[84,64,128]{2,1,0:T(8,128)(2,1)S(1)} %copy-done.1) | data formatting | bytes 2752512 | tf_op args[1]
  20.3 11.9 %all-reduce = s32[64]{0:T(128)S(1)} all-reduce(s32[64]{0:T(128)S(1)} %dynamic-update-slice), channel_id=1, replica_groups=mesh['band'=8,'lev'=4] {'band'}, use_global_device_ids=true, to_apply=%add | all-reduce | flops 64 | bytes 512
  32.5 19.2 %while.16 = (s32[]{:T(128)}, f32[128,128]{1,0:T(8,128)S(1)}, s32[64]{0:T(128)S(1)}, bf16[128,128]{1,0:T(8,128)(2,1)S(1)}, s32[]{:T(128)}, /*index=5*/s32[]{:T(128)}, s32[]{:T(128)}) while((s32[]{:T(128)}, f32[128,128]{1,0:T(8,128)S(1)}, s32[64]{0:T(128)S(1)}, bf16[128,128]{1,0:T(8,128)(2,1)S(1)}, s32[]{:T(128)}, ...), condition=%wide.region_2.3_spmd.clone, body=%wide.region_1.2_spmd.clone.sunk | while | flops 85623296 | bytes 3477863 | solution.py:61
  32.5 1.1 %fusion.69 = (f32[512,64]{1,0:T(8,128)S(1)}, f32[512,64]{1,0:T(8,128)S(1)}) fusion(s32[64]{0:T(128)S(1)} %get-tuple-element.210, s32[512]{0:T(512)S(1)} %iota_add_fusion.3), kind=kLoop, calls=%fused_computation.20.clone.1 | loop fusion | flops 491520 | bytes 264448 | tf_op jit(solution)/shard_map/while/body/eval_jaxpr/cos | solution.py:40
  34.9 1.1 %fusion.69 = (f32[512,64]{1,0:T(8,128)S(1)}, f32[512,64]{1,0:T(8,128)S(1)}) fusion(s32[64]{0:T(128)S(1)} %get-tuple-element.210, s32[512]{0:T(512)S(1)} %iota_add_fusion.3), kind=kLoop, calls=%fused_computation.20.clone.1 | loop fusion | flops 491520 | bytes 264448 | tf_op jit(solution)/shard_map/while/body/eval_jaxpr/cos | solution.py:40
  37.3 1.1 %fusion.69 = (f32[512,64]{1,0:T(8,128)S(1)}, f32[512,64]{1,0:T(8,128)S(1)}) fusion(s32[64]{0:T(128)S(1)} %get-tuple-element.210, s32[512]{0:T(512)S(1)} %iota_add_fusion.3), kind=kLoop, calls=%fused_computation.20.clone.1 | loop fusion | flops 491520 | bytes 264448 | tf_op jit(solution)/shard_map/while/body/eval_jaxpr/cos | solution.py:40
  39.7 1.1 %fusion.69 = (f32[512,64]{1,0:T(8,128)S(1)}, f32[512,64]{1,0:T(8,128)S(1)}) fusion(s32[64]{0:T(128)S(1)} %get-tuple-element.210, s32[512]{0:T(512)S(1)} %iota_add_fusion.3), kind=kLoop, calls=%fused_computation.20.clone.1 | loop fusion | flops 491520 | bytes 264448 | tf_op jit(solution)/shard_map/while/body/eval_jaxpr/cos | solution.py:40
  42.1 1.1 %fusion.69 = (f32[512,64]{1,0:T(8,128)S(1)}, f32[512,64]{1,0:T(8,128)S(1)}) fusion(s32[64]{0:T(128)S(1)} %get-tuple-element.210, s32[512]{0:T(512)S(1)} %iota_add_fusion.3), kind=kLoop, calls=%fused_computation.20.clone.1 | loop fusion | flops 491520 | bytes 264448 | tf_op jit(solution)/shard_map/while/body/eval_jaxpr/cos | solution.py:40
  44.5 1.1 %fusion.69 = (f32[512,64]{1,0:T(8,128)S(1)}, f32[512,64]{1,0:T(8,128)S(1)}) fusion(s32[64]{0:T(128)S(1)} %get-tuple-element.210, s32[512]{0:T(512)S(1)} %iota_add_fusion.3), kind=kLoop, calls=%fused_computation.20.clone.1 | loop fusion | flops 491520 | bytes 264448 | tf_op jit(solution)/shard_map/while/body/eval_jaxpr/cos | solution.py:40
  46.9 1.1 %fusion.69 = (f32[512,64]{1,0:T(8,128)S(1)}, f32[512,64]{1,0:T(8,128)S(1)}) fusion(s32[64]{0:T(128)S(1)} %get-tuple-element.210, s32[512]{0:T(512)S(1)} %iota_add_fusion.3), kind=kLoop, calls=%fused_computation.20.clone.1 | loop fusion | flops 491520 | bytes 264448 | tf_op jit(solution)/shard_map/while/body/eval_jaxpr/cos | solution.py:40
  49.3 1.1 %fusion.69 = (f32[512,64]{1,0:T(8,128)S(1)}, f32[512,64]{1,0:T(8,128)S(1)}) fusion(s32[64]{0:T(128)S(1)} %get-tuple-element.210, s32[512]{0:T(512)S(1)} %iota_add_fusion.3), kind=kLoop, calls=%fused_computation.20.clone.1 | loop fusion | flops 491520 | bytes 264448 | tf_op jit(solution)/shard_map/while/body/eval_jaxpr/cos | solution.py:40
  52.3 3.3 %all-to-all-start.1 = ((bf16[1,64,2,128]{3,2,0,1:T(2,128)(2,1)}), bf16[1,64,2,128]{3,2,0,1:T(2,128)(2,1)S(1)}, u32[]{:S(2)}, u32[]{:S(2)}) async-start(bf16[1,64,2,128]{3,2,0,1:T(2,128)(2,1)} %copy.108), calls=%async_computation.1 | async-start | bytes 65536 | tf_op jit(solution)/shard_map/all_to_all | solution.py:116
  55.7 6.6 %all-to-all-done.1 = bf16[1,64,2,128]{3,2,0,1:T(2,128)(2,1)S(1)} async-done(((bf16[1,64,2,128]{3,2,0,1:T(2,128)(2,1)}), bf16[1,64,2,128]{3,2,0,1:T(2,128)(2,1)S(1)}, u32[]{:S(2)}, u32[]{:S(2)}) %all-to-all-start.1) | async-done | bytes 32800 | tf_op jit(solution)/shard_map/all_to_all | solution.py:116
  62.3 0.7 reshape.129
  63.9 0.8 gather_fusion
  64.7 0.8 gather_fusion.1
  65.6 1.4 %select_bitcast_fusion.1 = (bf16[8,84,2,4,16]{4,0,3,2,1:T(8,128)(2,1)S(1)}, bf16[8,84,2,4,16]{4,0,3,2,1:T(8,128)(2,1)}) fusion(bf16[84,8,2,4,16]{4,1,3,2,0:T(8,128)(2,1)S(1)} %gather_fusion, pred[84]{0:T(512)(128)(4,1)S(1)} %compare_and_fusion, bf16[84,8,2,4,16]{4,1,3,2,0:T(8,128)(2,1)S(1)} %gather_fusion.1), kind=kLoop, calls=%fused_computation.34 | loop fusion | flops 172032 | bytes 688212 | tf_op jit(solution)/shard_map/jit(_take)/select_n | solution.py:132
  67.0 0.8 copy-done.2
  67.8 2.1 %fusion.16 = f32[84,4,2,1,32]{4,1,2,0,3:T(4,128)} fusion(bf16[84,64,8,16]{1,3,2,0:T(8,128)(2,1)S(1)} %bitcast.156, bf16[8,84,2,4,16]{4,0,3,2,1:T(8,128)(2,1)S(1)} %get-tuple-element.159), kind=kOutput, calls=%fused_computation.37 | convolution fusion | flops 5505024 | bytes 1634304 | tf_op jit(solution)/shard_map/gkclt,krgt->klcr/dot_general | solution.py:135
  69.9 1.1 %copy.116 = f32[84,4,2,1,32]{0,4,3,2,1:T(8,128)S(1)} copy(f32[84,4,2,1,32]{4,1,2,0,3:T(4,128)} %fusion.16) | data formatting | bytes 172032 | tf_op jit(solution)/shard_map/stack | solution.py:148
  71.0 4.1 %fusion.19 = f32[84,4,2,1,32]{4,1,2,0,3:T(4,128)} fusion(bf16[84,64,8,16]{1,3,2,0:T(8,128)(2,1)S(1)} %bitcast.157, bf16[8,84,2,4,16]{4,0,3,2,1:T(8,128)(2,1)} %get-tuple-element.160), kind=kOutput, calls=%fused_computation.38 | convolution fusion | flops 5505024 | bytes 1634304 | tf_op jit(solution)/shard_map/gkclt,krgt->klcr/dot_general | solution.py:141
  75.2 1.1 %copy.117 = f32[84,4,2,1,32]{0,4,3,2,1:T(8,128)S(1)} copy(f32[84,4,2,1,32]{4,1,2,0,3:T(4,128)} %fusion.19) | data formatting | bytes 172032 | tf_op jit(solution)/shard_map/stack | solution.py:148
  76.6 6.3 %all_gather.7 = bf16[84,16,128]{2,0,1:T(8,128)(2,1)S(1)} all-gather(bf16[84,4,128]{2,0,1:T(8,128)(2,1)S(1)} %copy.118), channel_id=1, replica_groups=mesh['band'=8,'lev'=4] {'lev'}, dimensions={1}, use_global_device_ids=true | all-gather | bytes 430080 | tf_op jit(solution)/shard_map/all_gather | solution.py:158
  83.3 1.8 %convolution_bitcast_fusion.1 = f32[84,4,128]{2,1,0:T(4,128)} fusion(f32[84,16,128]{2,1,0:T(8,128)S(1)} %fusion.15, f32[16,16]{1,0:T(8,128)} %param.22, s32[]{:T(128)S(6)} %select_n.49), kind=kOutput, calls=%fused_computation.39 | convolution fusion | flops 8257536 | bytes 862212 | tf_op jit(solution)/shard_map/la,kax->klx/dot_general | solution.py:167
  (115 shorter events, 15.6 us)
Async XLA Ops:
  0.0 82.8 %copy-start = (f32[16,16]{1,0:T(8,128)S(1)}, f32[16,16]{1,0:T(8,128)}, u32[]{:S(2)}) copy-start(f32[16,16]{1,0:T(8,128)} %param.21) | copy-start | bytes 3076
  6.3 9.6 %copy-start.5 = (s32[84]{0:T(128)S(1)}, s32[84]{0:T(128)}, u32[]{:S(2)}) copy-start(s32[84]{0:T(128)} %param.17) | copy-start | bytes 1012
  6.4 9.6 %copy-start.1 = (bf16[84,64,128]{2,1,0:T(8,128)(2,1)S(1)}, bf16[84,64,128]{2,1,0:T(8,128)(2,1)}, u32[]{:S(2)}) copy-start(bf16[84,64,128]{2,1,0:T(8,128)(2,1)} %param.15) | copy-start | bytes 4128772
  8.7 23.8 %all-to-all-start = ((bf16[8,8,2,128]{3,1,2,0:T(8,128)(2,1)}), bf16[8,8,2,128]{3,1,2,0:T(8,128)(2,1)S(1)}, u32[]{:S(2)}, u32[]{:S(2)}) async-start(bf16[8,8,2,128]{3,1,2,0:T(8,128)(2,1)} %convert_element_type.110), calls=%async_computation | async-start | bytes 65536 | tf_op jit(solution)/shard_map/all_to_all | solution.py:115
  16.0 2.7 %copy-start.9 = (u32[32]{0:T(128)S(1)}, u32[32]{0:T(128)}, u32[]{:S(2)}) copy-start(u32[32]{0:T(128)} %constant.121) | copy-start | bytes 388
  16.0 4.1 %copy-start.6 = (s32[8]{0:T(128)S(1)}, s32[8]{0:T(128)}, u32[]{:S(2)}) copy-start(s32[8]{0:T(128)} %param.16) | copy-start | bytes 100
  16.0 16.2 %copy-start.4 = (f32[4,2,128]{2,1,0:T(2,128)S(1)}, f32[4,2,128]{2,1,0:T(2,128)}, u32[]{:S(2)}) copy-start(f32[4,2,128]{2,1,0:T(2,128)} %param.20) | copy-start | bytes 12292
  16.0 16.2 %copy-start.7 = (f32[128]{0:T(128)S(1)}, f32[128]{0:T(128)}, u32[]{:S(2)}) copy-start(f32[128]{0:T(128)} %param.19) | copy-start | bytes 1540
  52.3 10.0 %all-to-all-start.1 = ((bf16[1,64,2,128]{3,2,0,1:T(2,128)(2,1)}), bf16[1,64,2,128]{3,2,0,1:T(2,128)(2,1)S(1)}, u32[]{:S(2)}, u32[]{:S(2)}) async-start(bf16[1,64,2,128]{3,2,0,1:T(2,128)(2,1)} %copy.108), calls=%async_computation.1 | async-start | bytes 65536 | tf_op jit(solution)/shard_map/all_to_all | solution.py:116
  65.5 2.3 %copy-start.2 = (bf16[84,64,128]{1,2,0:T(8,128)(2,1)S(1)}, bf16[84,64,128]{1,2,0:T(8,128)(2,1)}, u32[]{:S(2)}) copy-start(bf16[84,64,128]{1,2,0:T(8,128)(2,1)} %copy.113) | copy-start | bytes 4128772
  67.8 3.2 %copy-start.3 = (bf16[84,64,128]{1,2,0:T(8,128)(2,1)S(1)}, bf16[84,64,128]{1,2,0:T(8,128)(2,1)}, u32[]{:S(2)}) copy-start(bf16[84,64,128]{1,2,0:T(8,128)(2,1)} %copy.113) | copy-start | bytes 4128772
  75.2 7.6 %copy-start.8 = (f32[16]{0:T(128)S(1)}, f32[16]{0:T(128)}, u32[]{:S(2)}) copy-start(f32[16]{0:T(128)} %param.23) | copy-start | bytes 196
where the time goes:
time: 85.7 us; the launch traced here: 85.1 us
  blocking collectives  18.1 us (21%)
  matrix products  17.8 us (21%)
  other arithmetic  15.5 us (18%)
  local copies, waits for them, and re-layouts  14.7 us (17%)
  starting transfers between devices  10.6 us (12%)
  waiting for transfers between devices  6.61 us (8%)
  between operations  1.07 us (1%)
    unnamed x1, blocking collectives  11.9 us
    cos x8, other arithmetic, one_block(): twiddle = jnp.concatenate([jnp.cos(angles), -jnp.sin(angles)], axis=1)  8.82 us
    all_to_all x1, starting transfers between devices, on_device(): lax.all_to_all(outgoing, 'band', split_axis=0, concat_axis=1, tiled=True)  7.28 us
    all_to_all x1, waiting for transfers between devices, on_device(): lax.all_to_all(drag_columns(incoming, all_waves), 'band', split_axis=1, c...  6.61 us
    all_gather x1, blocking collectives, on_device(): lax.all_gather(combined.astype(jnp.bfloat16), 'lev', axis=1, tiled=True)  6.27 us
    unnamed x25, local copies, waits for them, and re-layouts  5.42 us
    dot_general x1, matrix products, on_device(): jnp.einsum('gkclt,krgt->klcr', anti_blocks, legendre_grid[:, half_rows:],...  4.15 us
    all_to_all x1, starting transfers between devices, on_device(): lax.all_to_all(drag_columns(incoming, all_waves), 'band', split_axis=1, c...  3.34 us
  transfers between devices with their start and end apart: 2, of which 1 were waited for; matrix products, arithmetic and copies ran while one was open for 4% of the time, Pallas kernels for 0%

commit v1 on v0

v1 whole, which is shorter than its diff:
```python
import functools
import math

import jax
import jax.numpy as jnp
from jax import lax
from jax.experimental import pallas as pl
from jax.experimental.pallas import tpu as pltpu
from jax.sharding import PartitionSpec as P

NTRUNC = 1280
NLON = 4096
LANES = 128
MESH = pl.DeviceIdType.MESH
NT = (((1,), (1,)), ((), ()))
F32 = jnp.float32
BF16 = jnp.bfloat16


def iota(shape, dim):
    return lax.broadcasted_iota(jnp.int32, shape, dim)


def whole_div(values, divisor):
    return jnp.floor((values.astype(F32) + 0.5) * (1.0 / divisor)).astype(jnp.int32)


def whole_mod(values, divisor):
    return values - divisor * whole_div(values, divisor)


def kernel(
    band_size,
    lev_size,
    chunk_blocks,
    waves_ref,
    slot_ref,
    start_ref,
    depth_ref,
    x_ref,
    leg_ref,
    weight_ref,
    drag_ref,
    inverse_ref,
    modes_ref,
    out_ref,
    wave_all,
    outgoing,
    incoming,
    leaving,
    returned,
    twiddle,
    picked,
    picks,
    degree,
    mixed,
    gathered,
    gain,
    wave_sems,
    go_sems,
    back_sems,
    lev_sems,
):
    band = lax.axis_index("band")
    lev = lax.axis_index("lev")
    block_count, row_count, lat_pairs = leg_ref.shape
    half = row_count // 2
    levels = x_ref.shape[0] // block_count
    all_levels = levels * lev_size
    slots = waves_ref.shape[0]
    pair = 2 * slots
    lat_chunks = lat_pairs // LANES
    wave_rows = band_size * pair
    chunks = block_count // chunk_blocks
    chunk_rows = chunk_blocks * levels

    barrier = pltpu.get_barrier_semaphore()
    for step in range(1, band_size):
        pl.semaphore_signal(
            barrier, inc=1, device_id={"band": lax.rem(band + step, band_size)}, device_id_type=MESH
        )
    for step in range(1, lev_size):
        pl.semaphore_signal(
            barrier, inc=1, device_id={"lev": lax.rem(lev + step, lev_size)}, device_id_type=MESH
        )

    row16 = iota((pair, LANES), 0)
    own_waves = jnp.zeros((pair, LANES), jnp.int32)
    for s in range(slots):
        own_waves = jnp.where((row16 == s) | (row16 == s + slots), waves_ref[s], own_waves)
    wave_all[band] = own_waves
    pl.semaphore_wait(barrier, band_size + lev_size - 2)

    def band_copies(source, target, sems, by_peer):
        copies = []
        for step in range(1, band_size):
            peer = lax.rem(band + step, band_size)
            copies.append(
                pltpu.make_async_remote_copy(
                    src_ref=source.at[peer] if by_peer else source.at[band],
                    dst_ref=target.at[band],
                    send_sem=sems.at[0, step],
                    recv_sem=sems.at[1, step],
                    device_id={"band": peer},
                    device_id_type=MESH,
                )
            )
        for copy in copies:
            copy.start()
        return copies

    wave_copies = band_copies(wave_all, wave_all, wave_sems, False)

    lane = iota((1, LANES), 1)
    in_row = jnp.where(lane < row_count, lane, lane - row_count)
    even_lane = in_row < half
    real_lane = lane < row_count
    offset = jnp.where(even_lane, 2 * in_row, 2 * (in_row - half) + 1)

    slot_row = iota((slots, LANES), 0)
    lane8 = iota((slots, LANES), 1)
    in8 = jnp.where(lane8 < row_count, lane8, lane8 - row_count)
    parts = [
        (lane8 < row_count) & (in8 < half),
        (lane8 >= row_count) & (in8 < half),
        (lane8 < row_count) & (in8 >= half),
        (lane8 >= row_count) & (in8 >= half),
    ]

    slot_degree = own_waves[:slots] + offset

    def forward_lhs(k, first):
        own = slot_row == slot_ref[k]
        reached = slot_degree + start_ref[k]
        if first:
            degree[pl.ds(k, 1), :] = jnp.sum(
                jnp.where(own, reached, 0).astype(F32), axis=0, keepdims=True
            )
        own = own & (reached < NTRUNC)
        pieces = []
        rows = [jnp.where(own, x_ref[pl.ds(k * levels + l, 1), :], 0.0) for l in range(levels)]
        for parity in range(2):
            for l in range(levels):
                for c in range(2):
                    pieces.append(jnp.where(parts[2 * parity + c], rows[l], 0.0))
        return jnp.concatenate(pieces, axis=0).astype(BF16)

    group = 4
    for ic in range(lat_chunks):
        cols = pl.ds(ic * LANES, LANES)

        def forward(g, total, cols=cols, first_pass=ic == 0):
            for u in range(0, group, 2):
                k = g * group + u
                lhs = jnp.concatenate(
                    [forward_lhs(k, first_pass), forward_lhs(k + 1, first_pass)], axis=1
                )
                first, second = leg_ref[k, :, cols], leg_ref[k + 1, :, cols]
                rhs = jnp.concatenate([first, first, second, second], axis=0)
                total = total + jnp.dot(lhs, rhs, preferred_element_type=F32)
            return total

        total = lax.fori_loop(
            0, block_count // group, forward, jnp.zeros((2 * levels * pair, LANES), F32)
        )
        for l in range(levels):
            even = total[l * pair : (l + 1) * pair]
            odd = total[(levels + l) * pair : (levels + l + 1) * pair]
            outgoing[(2 * l) * lat_chunks + ic] = (even + odd).astype(BF16)
            outgoing[(2 * l + 1) * lat_chunks + ic] = (even - odd).astype(BF16)
    go_copies = band_copies(outgoing, incoming, go_sems, True)
    incoming[band] = outgoing[band]

    for copy in wave_copies:
        copy.wait()
    turn = 2.0 * math.pi / NLON
    row_block = min(wave_rows, 128)
    peers_in = row_block // pair

    def twiddle_rows(t):
        wave = jnp.concatenate([wave_all[t * peers_in + p] for p in range(peers_in)], axis=0)
        lanes = iota((row_block, LANES), 1)
        real = (iota((row_block, LANES), 0) & (pair - 1)) < slots
        coarse = ((wave * lanes * LANES) & (NLON - 1)).astype(F32) * turn
        fine = ((wave * lanes) & (NLON - 1)).astype(F32) * turn
        cos_c, sin_c = jnp.cos(coarse), jnp.sin(coarse)
        lead, trail = jnp.where(real, cos_c, -sin_c), jnp.where(real, sin_c, cos_c)
        cos_f, sin_f = jnp.cos(fine), jnp.sin(fine)
        rows = pl.ds(t * row_block, row_block)
        for a in range(NLON // LANES):
            values = lead[:, a : a + 1] * cos_f - trail[:, a : a + 1] * sin_f
            twiddle[rows, pl.ds(a * LANES, LANES)] = values.astype(BF16)

    for t in range(wave_rows // row_block):
        twiddle_rows(t)
    for copy in go_copies:
        copy.wait()

    field = jnp.concatenate([incoming[p] for p in range(band_size)], axis=0)
    field = field.astype(F32).T.astype(BF16)
    width = 512

    def drag_block(j, total):
        cols = pl.ds(pl.multiple_of(j * width, width), width)
        table = twiddle[:, cols]
        values = jnp.dot(field, table, preferred_element_type=F32)
        force = (values * jnp.abs(values)).astype(BF16)
        return total + lax.dot_general(table, force, NT, preferred_element_type=F32)

    spectrum = lax.fori_loop(
        0, NLON // width, drag_block, jnp.zeros((wave_rows, LANES), F32), unroll=True
    )
    spectrum = (spectrum * (1.0 / (band_size * slots * math.sqrt(NLON)))).astype(BF16)
    for p in range(band_size):
        leaving[p] = spectrum[p * pair : (p + 1) * pair]
    back_copies = band_copies(leaving, returned, back_sems, True)
    returned[band] = leaving[band]

    modal_rows = chunk_blocks * all_levels
    r_of, c_of = iota((modal_rows, all_levels), 0), iota((modal_rows, all_levels), 1)
    spread = (whole_mod(r_of, all_levels) == c_of).astype(F32).astype(BF16)
    l_of, q_of = iota((all_levels, modal_rows), 0), iota((all_levels, modal_rows), 1)
    level_of = levels * whole_div(q_of, chunk_rows) + whole_mod(q_of, levels)
    collect = (l_of == level_of).astype(F32).astype(BF16)
    left = jnp.dot(spread, inverse_ref[...].astype(BF16), preferred_element_type=F32).astype(BF16)
    left = jnp.dot(left, collect, preferred_element_type=F32)
    r_of, c_of = iota((modal_rows, modal_rows), 0), iota((modal_rows, modal_rows), 1)
    same = whole_div(r_of, all_levels) == whole_div(whole_mod(c_of, chunk_rows), levels)
    to_modes = jnp.where(same, left, 0.0).astype(BF16)
    r_of, c_of = iota((chunk_rows, all_levels), 0), iota((chunk_rows, all_levels), 1)
    spread = (c_of == lev * levels + whole_mod(r_of, levels)).astype(F32).astype(BF16)
    collect = (l_of == whole_mod(q_of, all_levels)).astype(F32).astype(BF16)
    right = jnp.dot(spread, modes_ref[...].astype(BF16), preferred_element_type=F32).astype(BF16)
    right = jnp.dot(right, collect, preferred_element_type=F32)
    r_of, c_of = iota((chunk_rows, modal_rows), 0), iota((chunk_rows, modal_rows), 1)
    same = whole_div(r_of, levels) == whole_div(c_of, all_levels)
    from_modes = jnp.where(same, right, 0.0).astype(BF16)

    mode_row = iota((all_levels, LANES), 0)
    depth = jnp.zeros((all_levels, LANES), F32)
    for a in range(all_levels):
        depth = jnp.where(mode_row == a, depth_ref[a], depth)

    kinds = 4 * levels
    kind_lane = iota((kinds, kinds * slots), 1)
    lane_slot = whole_mod(kind_lane, slots)
    kind = whole_div(kind_lane, slots) == iota((kinds, kinds * slots), 0)

    def gain_block(g, carry):
        for u in range(group):
            k = g * group + u
            n = degree[pl.ds(k, 1), :]
            growth = n * (n + 1.0) * (1.0 / (NTRUNC * NTRUNC))
            rows = pl.ds(pl.multiple_of(k * all_levels, all_levels), all_levels)
            gain[rows, :] = 1.0 / (1.0 + depth * growth)
            rows = pl.ds(pl.multiple_of(k * 4 * levels, 16), 4 * levels)
            picks[rows, :] = jnp.where(kind & (lane_slot == slot_ref[k]), 1.0, 0.0).astype(BF16)
        return carry

    lax.fori_loop(0, block_count // group, gain_block, 0)
    for copy in back_copies:
        copy.wait()

    for ic in range(lat_chunks):
        columns = [None] * kinds
        weight = -weight_ref[:, ic * LANES : (ic + 1) * LANES]
        for l in range(levels):
            north = returned[(2 * l) * lat_chunks + ic].astype(F32)
            south = returned[(2 * l + 1) * lat_chunks + ic].astype(F32)
            drag_n = drag_ref[2 * l : 2 * l + 1, ic * LANES : (ic + 1) * LANES]
            drag_s = drag_ref[2 * l + 1 : 2 * l + 2, ic * LANES : (ic + 1) * LANES]
            north, south = drag_n * north, drag_s * south
            for parity, value in enumerate((weight * (north + south), weight * (north - south))):
                for c in range(2):
                    at = (parity * 2 + c) * levels + l
                    columns[at] = value[c * slots : (c + 1) * slots]

        picked[ic] = jnp.concatenate(columns, axis=0).astype(BF16)

    def lev_copies(j):
        rows = pl.ds(pl.multiple_of(j * chunk_rows, chunk_rows), chunk_rows)
        return [
            pltpu.make_async_remote_copy(
                src_ref=gathered.at[lev, rows],
                dst_ref=gathered.at[lev, rows],
                send_sem=lev_sems.at[0, step, j],
                recv_sem=lev_sems.at[1, step, j],
                device_id={"lev": lax.rem(lev + step, lev_size)},
                device_id_type=MESH,
            )
            for step in range(1, lev_size)
        ]

    def direct_chunk(j, carry):
        pick_rows = pl.ds(pl.multiple_of(j * chunk_blocks * kinds, 16), chunk_blocks * kinds)
        chosen_rows = [
            jnp.dot(picks[pick_rows, :], picked[ic], preferred_element_type=F32).astype(BF16)
            for ic in range(lat_chunks)
        ]
        for u in range(0, chunk_blocks, 2):
            k = j * chunk_blocks + u
            product = None
            for ic in range(lat_chunks):
                cols = pl.ds(ic * LANES, LANES)
                lhs = chosen_rows[ic][u * kinds : (u + 2) * kinds]
                first, second = leg_ref[k, :, cols], leg_ref[k + 1, :, cols]
                rhs = jnp.concatenate([first, first, second, second], axis=0)
                term = lax.dot_general(lhs, rhs, NT, preferred_element_type=F32)
                product = term if product is None else product + term
            for v in range(2):
                own = product[v * 4 * levels : (v + 1) * 4 * levels, v * LANES : (v + 1) * LANES]
                chosen = jnp.where(even_lane, own[: 2 * levels], own[2 * levels :])
                tendency = jnp.where(real_lane, chosen[:levels], chosen[levels:])
                live = degree[pl.ds(k + v, 1), :] < NTRUNC
                rows = pl.ds((k + v) * levels, levels)
                mixed[rows, :] = jnp.where(live, x_ref[rows, :] + tendency, 0.0)
        rows = pl.ds(pl.multiple_of(j * chunk_rows, chunk_rows), chunk_rows)
        gathered[lev, rows, :] = mixed[rows, :].astype(BF16)
        for copy in lev_copies(j):
            copy.start()
        return carry

    lax.fori_loop(0, chunks, direct_chunk, 0)

    def solve_chunk(j, carry):
        for copy in lev_copies(j):
            copy.wait()
        rows = pl.ds(pl.multiple_of(j * chunk_rows, chunk_rows), chunk_rows)
        columns = jnp.concatenate([gathered[q, rows, :] for q in range(lev_size)], axis=0)
        modal = jnp.dot(to_modes, columns, preferred_element_type=F32)
        gains = gain[pl.ds(pl.multiple_of(j * modal_rows, modal_rows), modal_rows), :]
        out_ref[rows, :] = jnp.dot(
            from_modes, (modal * gains).astype(BF16), preferred_element_type=F32
        )
        return carry

    lax.fori_loop(0, chunks, solve_chunk, 0)


def on_device(band_size, lev_size, *args):
    spectral, legendre, waves, slot, start, weights, drag, inverse, modes, depths = args
    block_count, levels, columns = spectral.shape
    lat_pairs = legendre.shape[2]
    slots, all_levels = waves.shape[0], inverse.shape[0]
    pair = 2 * slots
    rows = block_count * levels
    chunk_blocks = max(
        n
        for n in range(2, 17, 2)
        if block_count % n == 0 and n * levels % 16 == 0
    )
    chunks = block_count // chunk_blocks
    assert levels * 2 * lat_pairs == band_size * LANES and columns == LANES
    smem = pl.BlockSpec(memory_space=pltpu.SMEM)
    vmem = pl.BlockSpec(memory_space=pltpu.VMEM)
    box = (band_size, pair, LANES)
    result = pl.pallas_call(
        functools.partial(kernel, band_size, lev_size, chunk_blocks),
        out_shape=jax.ShapeDtypeStruct((rows, LANES), F32),
        in_specs=[smem] * 4 + [vmem] * 6,
        out_specs=vmem,
        scratch_shapes=[
            pltpu.VMEM(box, jnp.int32),
            pltpu.VMEM(box, BF16),
            pltpu.VMEM(box, BF16),
            pltpu.VMEM(box, BF16),
            pltpu.VMEM(box, BF16),
            pltpu.VMEM((band_size * pair, NLON), BF16),
            pltpu.VMEM((lat_pairs // LANES, slots * 4 * levels, LANES), BF16),
            pltpu.VMEM((rows * 4, slots * 4 * levels), BF16),
            pltpu.VMEM((block_count, LANES), F32),
            pltpu.VMEM((rows, LANES), F32),
            pltpu.VMEM((lev_size, rows, LANES), BF16),
            pltpu.VMEM((block_count * all_levels, LANES), F32),
            pltpu.SemaphoreType.DMA((2, band_size)),
            pltpu.SemaphoreType.DMA((2, band_size)),
            pltpu.SemaphoreType.DMA((2, band_size)),
            pltpu.SemaphoreType.DMA((2, lev_size, chunks)),
        ],
        compiler_params=pltpu.CompilerParams(
            collective_id=0, has_side_effects=True, vmem_limit_bytes=48 * 2**20
        ),
    )(
        waves,
        slot,
        start,
        depths,
        spectral.reshape(rows, LANES),
        legendre,
        weights.reshape(1, lat_pairs),
        drag.reshape(levels * 2, lat_pairs),
        inverse,
        modes,
    )
    return result.reshape(spectral.shape)


def solution(mesh):
    placed = (
        P("band", "lev", None),
        P("band", None, None),
        P("band"),
        P("band"),
        P("band"),
        P(),
        P("lev", None, None),
        P(),
        P(),
        P(),
    )
    return jax.shard_map(
        functools.partial(on_device, mesh.shape["band"], mesh.shape["lev"]),
        mesh=mesh,
        in_specs=placed,
        out_specs=P("band", "lev", None),
        check_vma=False,
    )
```

time: 85.7 us -> 34.9 us (0.41)
  Pallas kernels: 0 us -> 26.3 us
  blocking collectives: 18.1 us -> 0 us
  matrix products: 17.8 us -> 0 us
  other arithmetic: 15.5 us -> 0 us
  starting transfers between devices: 10.6 us -> 0 us
  waiting for transfers between devices: 6.61 us -> 0 us
  local copies, waits for them, and re-layouts: 14.7 us -> 8.28 us
  between operations: 1.07 us -> 0.02 us
    pallas_call x0 -> x1, Pallas kernels: none -> 26.3 us  [on_device(): pl.pallas_call(functools.partial(kernel, band_size, lev_size, chunk_block...]
    dot_general x46 -> x0, matrix products: 17.8 us -> none  [the longest x1 4.15 us: on_device(): jnp.einsum('gkclt,krgt->klcr', anti_blocks, legendre_grid[:, half_rows:],...]
    unnamed x1 -> x0, blocking collectives: 11.9 us -> none
    all_to_all x2 -> x0, starting transfers between devices: 10.6 us -> none  [the longest x1 7.28 us: on_device(): lax.all_to_all(outgoing, 'band', split_axis=0, concat_axis=1, tiled=True)]
    cos x8 -> x0, other arithmetic: 8.82 us -> none  [one_block(): twiddle = jnp.concatenate([jnp.cos(angles), -jnp.sin(angles)], axis=1)]
    all_to_all x2 -> x0, waiting for transfers between devices: 6.61 us -> none  [the longest x1 6.61 us: on_device(): lax.all_to_all(drag_columns(incoming, all_waves), 'band', split_axis=1, c...]
    all_gather x1 -> x0, blocking collectives: 6.27 us -> none  [on_device(): lax.all_gather(combined.astype(jnp.bfloat16), 'lev', axis=1, tiled=True)]
    another operation x8 -> x0, local copies, waits for them, and re-layouts: 3.66 us -> none  [the longest x2 2.25 us: on_device(): jnp.stack([even_tend, odd_tend], axis=3)]
  transfers between devices with their start and end apart: 2 -> 0, of which waited for: 1 -> 0; matrix products, arithmetic and copies ran while one was open for 4% -> 0% of each run, Pallas kernels for 0% -> 0%
where the time goes in v1:
time: 34.9 us; the launch traced here: 34.6 us
  Pallas kernels  26.3 us (75%)
  local copies, waits for them, and re-layouts  8.28 us (24%)
    pallas_call x1, Pallas kernels, on_device(): pl.pallas_call(functools.partial(kernel, band_size, lev_size, chunk_block...  26.3 us
    unnamed x21, local copies, waits for them, and re-layouts  8.28 us

profile of v1, /device:TPU:0, one launch (start us, length us, event | category | flops | bytes accessed | tf_op | source)
XLA Modules:
  0.0 34.6 jit_solution(16887184196644722456)
XLA Ops:
  0.0 0.0 copy-start
  0.0 1.3 %copy-done = bf16[84,64,128]{2,1,0:T(8,128)(2,1)S(1)} copy-done((bf16[84,64,128]{2,1,0:T(8,128)(2,1)S(1)}, bf16[84,64,128]{2,1,0:T(8,128)(2,1)}, u32[]{:S(2)}) %copy-start) | copy-done | bytes 1376280
  1.3 0.0 copy-start.1
  1.3 0.9 %copy-done.1 = f32[84,4,128]{2,1,0:T(4,128)S(1)} copy-done((f32[84,4,128]{2,1,0:T(4,128)S(1)}, f32[84,4,128]{2,1,0:T(4,128)}, u32[]{:S(2)}) %copy-start.1) | copy-done | bytes 172056
  2.3 0.0 copy-start.2
  2.3 0.7 %copy-done.2 = f32[16,16]{1,0:T(8,128)S(1)} copy-done((f32[16,16]{1,0:T(8,128)S(1)}, f32[16,16]{1,0:T(8,128)}, u32[]{:S(2)}) %copy-start.2) | copy-done | bytes 1048
  3.0 0.0 copy-start.3
  3.0 0.7 %copy-done.3 = f32[16,16]{1,0:T(8,128)S(1)} copy-done((f32[16,16]{1,0:T(8,128)S(1)}, f32[16,16]{1,0:T(8,128)}, u32[]{:S(2)}) %copy-start.3) | copy-done | bytes 1048
  3.7 0.0 copy-start.4
  3.7 0.7 %copy-done.4 = f32[4,2,128]{2,1,0:T(2,128)S(1)} copy-done((f32[4,2,128]{2,1,0:T(2,128)S(1)}, f32[4,2,128]{2,1,0:T(2,128)}, u32[]{:S(2)}) %copy-start.4) | copy-done | bytes 4120
  4.3 0.0 copy-start.5
  4.3 0.7 %copy-done.5 = s32[8]{0:T(128)S(1)} copy-done((s32[8]{0:T(128)S(1)}, s32[8]{0:T(128)}, u32[]{:S(2)}) %copy-start.5) | copy-done | bytes 56
  5.0 0.0 copy-start.6
  5.0 0.7 %copy-done.6 = s32[84]{0:T(128)S(1)} copy-done((s32[84]{0:T(128)S(1)}, s32[84]{0:T(128)}, u32[]{:S(2)}) %copy-start.6) | copy-done | bytes 360
  5.7 0.0 copy-start.7
  5.7 0.7 %copy-done.7 = s32[84]{0:T(128)S(1)} copy-done((s32[84]{0:T(128)S(1)}, s32[84]{0:T(128)}, u32[]{:S(2)}) %copy-start.7) | copy-done | bytes 360
  6.3 0.0 copy-start.8
  6.3 0.7 %copy-done.8 = f32[16]{0:T(128)S(1)} copy-done((f32[16]{0:T(128)S(1)}, f32[16]{0:T(128)}, u32[]{:S(2)}) %copy-start.8) | copy-done | bytes 88
  7.0 0.0 copy-start.9
  7.0 0.7 %copy-done.9 = f32[128]{0:T(128)S(1)} copy-done((f32[128]{0:T(128)S(1)}, f32[128]{0:T(128)}, u32[]{:S(2)}) %copy-start.9) | copy-done | bytes 536
  7.6 26.3 %shard_map.100 = f32[336,128]{1,0:T(8,128)S(1)} custom-call(s32[8]{0:T(128)S(1)} %copy-done.5, s32[84]{0:T(128)S(1)} %copy-done.6, s32[84]{0:T(128)S(1)} %copy-done.7, f32[16]{0:T(128)S(1)} %copy-done.8, f32[336,128]{1,0:T(8,128)S(1)} %bitcast.5, bf16[84,64,128]{2,1,0:T(8,128)(2,1)S(1)} %copy-done, f32[1,128]{1,0:T(1,128)S(1)} %bitcast.7, ...), custom_call_target="tpu_custom_call" | custom-call | tf_op jit(solution)/shard_map/pallas_call | solution.py:357
  33.9 0.7 %copy.12 = f32[84,4,128]{2,1,0:T(4,128)} copy(f32[84,4,128]{2,1,0:T(4,128)S(1)} %bitcast.4) | data formatting | bytes 344064
Async XLA Ops:
  0.0 1.3 %copy-start = (bf16[84,64,128]{2,1,0:T(8,128)(2,1)S(1)}, bf16[84,64,128]{2,1,0:T(8,128)(2,1)}, u32[]{:S(2)}) copy-start(bf16[84,64,128]{2,1,0:T(8,128)(2,1)} %leg_ref.1) | copy-start | bytes 4128772
  1.3 0.9 %copy-start.1 = (f32[84,4,128]{2,1,0:T(4,128)S(1)}, f32[84,4,128]{2,1,0:T(4,128)}, u32[]{:S(2)}) copy-start(f32[84,4,128]{2,1,0:T(4,128)} %param.10) | copy-start | bytes 516100
  2.3 0.7 %copy-start.2 = (f32[16,16]{1,0:T(8,128)S(1)}, f32[16,16]{1,0:T(8,128)}, u32[]{:S(2)}) copy-start(f32[16,16]{1,0:T(8,128)} %inverse_ref.1) | copy-start | bytes 3076
  3.0 0.7 %copy-start.3 = (f32[16,16]{1,0:T(8,128)S(1)}, f32[16,16]{1,0:T(8,128)}, u32[]{:S(2)}) copy-start(f32[16,16]{1,0:T(8,128)} %modes_ref.1) | copy-start | bytes 3076
  3.7 0.7 %copy-start.4 = (f32[4,2,128]{2,1,0:T(2,128)S(1)}, f32[4,2,128]{2,1,0:T(2,128)}, u32[]{:S(2)}) copy-start(f32[4,2,128]{2,1,0:T(2,128)} %param.16) | copy-start | bytes 12292
  4.3 0.7 %copy-start.5 = (s32[8]{0:T(128)S(1)}, s32[8]{0:T(128)}, u32[]{:S(2)}) copy-start(s32[8]{0:T(128)} %waves_ref.1) | copy-start | bytes 100
  5.0 0.7 %copy-start.6 = (s32[84]{0:T(128)S(1)}, s32[84]{0:T(128)}, u32[]{:S(2)}) copy-start(s32[84]{0:T(128)} %slot_ref.1) | copy-start | bytes 1012
  5.7 0.7 %copy-start.7 = (s32[84]{0:T(128)S(1)}, s32[84]{0:T(128)}, u32[]{:S(2)}) copy-start(s32[84]{0:T(128)} %start_ref.1) | copy-start | bytes 1012
  6.3 0.7 %copy-start.8 = (f32[16]{0:T(128)S(1)}, f32[16]{0:T(128)}, u32[]{:S(2)}) copy-start(f32[16]{0:T(128)} %depth_ref.1) | copy-start | bytes 196
  7.0 0.7 %copy-start.9 = (f32[128]{0:T(128)S(1)}, f32[128]{0:T(128)}, u32[]{:S(2)}) copy-start(f32[128]{0:T(128)} %param.15) | copy-start | bytes 1540

commit v2 on v1

--- a/solution.py
+++ b/solution.py
@@ -29,20 +29,32 @@
     return values - divisor * whole_div(values, divisor)
 
 
+def turns(phase):
+    phase = ((phase + NLON // 2) & (NLON - 1)) - NLON // 2
+    y = phase.astype(F32) * (math.pi / NLON)
+    z = y * y
+    sine, cosine = jnp.zeros_like(z), jnp.zeros_like(z)
+    for n in reversed(range(7)):
+        sine = sine * z + (-1) ** n / math.factorial(2 * n + 1)
+        cosine = cosine * z + (-1) ** n / math.factorial(2 * n)
+    sine = sine * y
+    return 1.0 - 2.0 * sine * sine, 2.0 * sine * cosine
+
+
 def kernel(
     band_size,
     lev_size,
     chunk_blocks,
-    waves_ref,
-    slot_ref,
-    start_ref,
-    depth_ref,
-    x_ref,
-    leg_ref,
-    weight_ref,
-    drag_ref,
-    inverse_ref,
-    modes_ref,
+    waves_hbm,
+    slot_hbm,
+    start_hbm,
+    depth_hbm,
+    x_hbm,
+    leg_hbm,
+    weight_hbm,
+    drag_hbm,
+    inverse_hbm,
+    modes_hbm,
     out_ref,
     wave_all,
     outgoing,
@@ -56,6 +68,17 @@
     mixed,
     gathered,
     gain,
+    waves_ref,
+    slot_ref,
+    start_ref,
+    depth_ref,
+    x_ref,
+    leg_ref,
+    weight_ref,
+    drag_ref,
+    inverse_ref,
+    modes_ref,
+    load_sems,
     wave_sems,
     go_sems,
     back_sems,
@@ -74,6 +97,23 @@
     chunks = block_count // chunk_blocks
     chunk_rows = chunk_blocks * levels
 
+    loads = [
+        pltpu.make_async_copy(source, target, load_sems.at[n])
+        for n, (source, target) in enumerate(
+            (
+                (waves_hbm, waves_ref),
+                (slot_hbm, slot_ref),
+                (start_hbm, start_ref),
+                (x_hbm, x_ref),
+                (leg_hbm, leg_ref),
+                (depth_hbm, depth_ref),
+                (weight_hbm, weight_ref),
+                (drag_hbm, drag_ref),
+                (inverse_hbm, inverse_ref),
+                (modes_hbm, modes_ref),
+            )
+        )
+    ]
     barrier = pltpu.get_barrier_semaphore()
     for step in range(1, band_size):
         pl.semaphore_signal(
@@ -84,6 +124,9 @@
             barrier, inc=1, device_id={"lev": lax.rem(lev + step, lev_size)}, device_id_type=MESH
         )
 
+    for load in loads:
+        load.start()
+    loads[0].wait()
     row16 = iota((pair, LANES), 0)
     own_waves = jnp.zeros((pair, LANES), jnp.int32)
     for s in range(slots):
@@ -110,6 +153,8 @@
         return copies
 
     wave_copies = band_copies(wave_all, wave_all, wave_sems, False)
+    for load in loads[1:]:
+        load.wait()
 
     lane = iota((1, LANES), 1)
     in_row = jnp.where(lane < row_count, lane, lane - row_count)
@@ -145,7 +190,7 @@
                     pieces.append(jnp.where(parts[2 * parity + c], rows[l], 0.0))
         return jnp.concatenate(pieces, axis=0).astype(BF16)
 
-    group = 4
+    group = chunk_blocks
     for ic in range(lat_chunks):
         cols = pl.ds(ic * LANES, LANES)
 
@@ -173,7 +218,6 @@
 
     for copy in wave_copies:
         copy.wait()
-    turn = 2.0 * math.pi / NLON
     row_block = min(wave_rows, 128)
     peers_in = row_block // pair
 
@@ -181,11 +225,9 @@
         wave = jnp.concatenate([wave_all[t * peers_in + p] for p in range(peers_in)], axis=0)
         lanes = iota((row_block, LANES), 1)
         real = (iota((row_block, LANES), 0) & (pair - 1)) < slots
-        coarse = ((wave * lanes * LANES) & (NLON - 1)).astype(F32) * turn
-        fine = ((wave * lanes) & (NLON - 1)).astype(F32) * turn
-        cos_c, sin_c = jnp.cos(coarse), jnp.sin(coarse)
+        cos_c, sin_c = turns(wave * lanes * LANES)
         lead, trail = jnp.where(real, cos_c, -sin_c), jnp.where(real, sin_c, cos_c)
-        cos_f, sin_f = jnp.cos(fine), jnp.sin(fine)
+        cos_f, sin_f = turns(wave * lanes)
         rows = pl.ds(t * row_block, row_block)
         for a in range(NLON // LANES):
             values = lead[:, a : a + 1] * cos_f - trail[:, a : a + 1] * sin_f
@@ -246,6 +288,8 @@
     lane_slot = whole_mod(kind_lane, slots)
     kind = whole_div(kind_lane, slots) == iota((kinds, kinds * slots), 0)
 
+    group = 4 if block_count % 4 == 0 else 2
+
     def gain_block(g, carry):
         for u in range(group):
             k = g * group + u
@@ -278,7 +322,8 @@
         picked[ic] = jnp.concatenate(columns, axis=0).astype(BF16)
 
     def lev_copies(j):
-        rows = pl.ds(pl.multiple_of(j * chunk_rows, chunk_rows), chunk_rows)
+        first = j * chunk_rows
+        rows = pl.ds(first if isinstance(j, int) else pl.multiple_of(first, chunk_rows), chunk_rows)
         return [
             pltpu.make_async_remote_copy(
                 src_ref=gathered.at[lev, rows],
@@ -322,19 +367,22 @@
 
     lax.fori_loop(0, chunks, direct_chunk, 0)
 
-    def solve_chunk(j, carry):
-        for copy in lev_copies(j):
-            copy.wait()
-        rows = pl.ds(pl.multiple_of(j * chunk_rows, chunk_rows), chunk_rows)
+    def solve_chunk(j):
+        rows = pl.ds(j * chunk_rows, chunk_rows)
         columns = jnp.concatenate([gathered[q, rows, :] for q in range(lev_size)], axis=0)
         modal = jnp.dot(to_modes, columns, preferred_element_type=F32)
-        gains = gain[pl.ds(pl.multiple_of(j * modal_rows, modal_rows), modal_rows), :]
+        gains = gain[pl.ds(j * modal_rows, modal_rows), :]
         out_ref[rows, :] = jnp.dot(
             from_modes, (modal * gains).astype(BF16), preferred_element_type=F32
         )
-        return carry
-
-    lax.fori_loop(0, chunks, solve_chunk, 0)
+
+    middle = (chunks + 1) // 2
+    for part in (range(middle), range(middle, chunks)):
+        for j in part:
+            for copy in lev_copies(j):
+                copy.wait()
+        for j in part:
+            solve_chunk(j)
 
 
 def on_device(band_size, lev_size, *args):
@@ -351,13 +399,12 @@
     )
     chunks = block_count // chunk_blocks
     assert levels * 2 * lat_pairs == band_size * LANES and columns == LANES
-    smem = pl.BlockSpec(memory_space=pltpu.SMEM)
     vmem = pl.BlockSpec(memory_space=pltpu.VMEM)
     box = (band_size, pair, LANES)
     result = pl.pallas_call(
         functools.partial(kernel, band_size, lev_size, chunk_blocks),
         out_shape=jax.ShapeDtypeStruct((rows, LANES), F32),
-        in_specs=[smem] * 4 + [vmem] * 6,
+        in_specs=[pl.BlockSpec(memory_space=pltpu.HBM)] * 10,
         out_specs=vmem,
         scratch_shapes=[
             pltpu.VMEM(box, jnp.int32),
@@ -372,13 +419,24 @@
             pltpu.VMEM((rows, LANES), F32),
             pltpu.VMEM((lev_size, rows, LANES), BF16),
             pltpu.VMEM((block_count * all_levels, LANES), F32),
+            pltpu.SMEM(waves.shape, jnp.int32),
+            pltpu.SMEM(slot.shape, jnp.int32),
+            pltpu.SMEM(start.shape, jnp.int32),
+            pltpu.SMEM(depths.shape, F32),
+            pltpu.VMEM((rows, LANES), F32),
+            pltpu.VMEM(legendre.shape, BF16),
+            pltpu.VMEM((1, lat_pairs), F32),
+            pltpu.VMEM((levels * 2, lat_pairs), F32),
+            pltpu.VMEM(inverse.shape, F32),
+            pltpu.VMEM(modes.shape, F32),
+            pltpu.SemaphoreType.DMA((10,)),
             pltpu.SemaphoreType.DMA((2, band_size)),
             pltpu.SemaphoreType.DMA((2, band_size)),
             pltpu.SemaphoreType.DMA((2, band_size)),
             pltpu.SemaphoreType.DMA((2, lev_size, chunks)),
         ],
         compiler_params=pltpu.CompilerParams(
-            collective_id=0, has_side_effects=True, vmem_limit_bytes=48 * 2**20
+            collective_id=0, has_side_effects=True, vmem_limit_bytes=60 * 2**20
         ),
     )(
         waves,

time: 34.9 us -> 26.7 us (0.77)
  local copies, waits for them, and re-layouts: 8.28 us -> 1.6 us
  Pallas kernels: 26.3 us -> 25 us
    unnamed x21 -> x1, local copies, waits for them, and re-layouts: 8.28 us -> 1.6 us
    pallas_call x1, Pallas kernels: 26.3 us -> 25 us  [on_device(): pl.pallas_call(functools.partial(kernel, band_size, lev_size, chunk_block...]
where the time goes in v2:
time: 26.7 us; the launch traced here: 26.6 us
  Pallas kernels  25 us (94%)
  local copies, waits for them, and re-layouts  1.6 us (6%)
    pallas_call x1, Pallas kernels, on_device(): pl.pallas_call(functools.partial(kernel, band_size, lev_size, chunk_block...  25 us
    unnamed x1, local copies, waits for them, and re-layouts  1.6 us

profile of v2, /device:TPU:0, one launch (start us, length us, event | category | flops | bytes accessed | tf_op | source)
XLA Modules:
  0.0 26.6 jit_solution(2836454055141934428)
XLA Ops:
  0.0 25.0 %shard_map.100 = f32[336,128]{1,0:T(8,128)} custom-call(s32[8]{0:T(128)} %waves_hbm.1, s32[84]{0:T(128)} %slot_hbm.1, s32[84]{0:T(128)} %start_hbm.1, f32[16]{0:T(128)} %depth_hbm.1, f32[336,128]{1,0:T(8,128)} %bitcast.5, bf16[84,64,128]{2,1,0:T(8,128)(2,1)} %leg_hbm.1, f32[1,128]{1,0:T(1,128)} %bitcast.7, f32[8,128]{1,0:T(8,128)} %bitcast.6, ...), custom_call_target="tpu_custom_call" | custom-call | tf_op jit(solution)/shard_map/pallas_call | solution.py:404
  25.0 1.6 %copy.12 = f32[84,4,128]{2,1,0:T(4,128)} copy(f32[84,4,128]{2,1,0:T(4,128)} %bitcast.4) | data formatting | bytes 344064

commit v3 on v2

--- a/solution.py
+++ b/solution.py
@@ -206,7 +206,8 @@
             return total
 
         total = lax.fori_loop(
-            0, block_count // group, forward, jnp.zeros((2 * levels * pair, LANES), F32)
+            0, block_count // group, forward, jnp.zeros((2 * levels * pair, LANES), F32),
+            unroll=lat_chunks == 1,
         )
         for l in range(levels):
             even = total[l * pair : (l + 1) * pair]
@@ -301,7 +302,7 @@
             picks[rows, :] = jnp.where(kind & (lane_slot == slot_ref[k]), 1.0, 0.0).astype(BF16)
         return carry
 
-    lax.fori_loop(0, block_count // group, gain_block, 0)
+    lax.fori_loop(0, block_count // group, gain_block, 0, unroll=3)
     for copy in back_copies:
         copy.wait()
 
@@ -377,7 +378,7 @@
         )
 
     middle = (chunks + 1) // 2
-    for part in (range(middle), range(middle, chunks)):
+    for part in (range(0, 3), range(3, 5), range(5, chunks)):
         for j in part:
             for copy in lev_copies(j):
                 copy.wait()

time: 26.7 us -> 26.3 us (0.985)
  Pallas kernels: 25 us -> 24.5 us
    pallas_call x1, Pallas kernels: 25 us -> 24.5 us  [on_device(): pl.pallas_call(functools.partial(kernel, band_size, lev_size, chunk_block...]
where the time goes in v3:
time: 26.3 us; the launch traced here: 26.2 us
  Pallas kernels  24.5 us (93%)
  local copies, waits for them, and re-layouts  1.6 us (6%)
    pallas_call x1, Pallas kernels, on_device(): pl.pallas_call(functools.partial(kernel, band_size, lev_size, chunk_block...  24.5 us
    unnamed x1, local copies, waits for them, and re-layouts  1.6 us

profile of v3, /device:TPU:0, one launch (start us, length us, event | category | flops | bytes accessed | tf_op | source)
XLA Modules:
  0.0 26.2 jit_solution(6829807930079986425)
XLA Ops:
  0.0 24.5 %shard_map.100 = f32[336,128]{1,0:T(8,128)} custom-call(s32[8]{0:T(128)} %waves_hbm.1, s32[84]{0:T(128)} %slot_hbm.1, s32[84]{0:T(128)} %start_hbm.1, f32[16]{0:T(128)} %depth_hbm.1, f32[336,128]{1,0:T(8,128)} %bitcast.5, bf16[84,64,128]{2,1,0:T(8,128)(2,1)} %leg_hbm.1, f32[1,128]{1,0:T(1,128)} %bitcast.7, f32[8,128]{1,0:T(8,128)} %bitcast.6, ...), custom_call_target="tpu_custom_call" | custom-call | tf_op jit(solution)/shard_map/pallas_call | solution.py:405
  24.6 1.6 %copy.12 = f32[84,4,128]{2,1,0:T(4,128)} copy(f32[84,4,128]{2,1,0:T(4,128)} %bitcast.4) | data formatting | bytes 344064
